TPU v7x, 128 devices: a whole 4x4x4 slice. The times are simulated.
128 devices in a mesh: group: 8 (over z, core), local: 16 (over y, x).
Axes of the slice: x: 4, y: 4, z: 4, core: 2. Of those that a mesh axis runs over, the one named last changes fastest.
Arguments:
- tokens: bfloat16 [512, 7168], P('local'), may hold values from -6 to 6
- cotangent: bfloat16 [512, 7168], P('local'), may hold values from -6 to 6
- gate_logits: float32 [512, 24], P('local'), may hold values from -8 to 8
- route_slot: int32 [512, 8], P('local'), may hold values from 0 to 31, all different within a row; in each aligned block of 32 rows (0 to 31, 32 to 63, ...) at most 16 rows name the same one
- slot_expert: int32 [32], replicated, may hold values from 0 to 23, as said below
- w_gate: bfloat16 [32, 7168, 1024], P('local', None, 'group')
- w_up: bfloat16 [32, 7168, 1024], P('local', None, 'group')
- w_down: bfloat16 [32, 1024, 7168], P('local', 'group'), as said below
Outputs:
- mixed: bfloat16 [512, 7168], P('local', 'group')
- grad_tokens: bfloat16 [512, 7168], P('local', 'group')
- grad_logits: float32 [512, 24], P('local')
- grad_gate: bfloat16 [32, 7168, 1024], P('local', None, 'group')
- grad_up: bfloat16 [32, 7168, 1024], P('local', None, 'group')
- grad_down: bfloat16 [32, 1024, 7168], P('local', 'group')
Inputs may be any that keep to these rules, and one draw needn't show every extreme that they name: `route_slot`: each token names 8 different slots. Of the 32 tokens of one index of local, at most 16 name one slot, a bound that some block reaches of them. `slot_expert`: the even slots hold 16 different experts, the odd slots the remaining ones, each on two odd slots: slot 2i + 1 and slot 2j + 1 hold the same expert where j = i plus or minus half the size of local (the one that stays in range). Every expert is held. `w_down`: two odd slots that hold the same expert have equal weights; entries have standard deviation 1024 ** -0.5.
All inputs are finite; a program needn't handle non-finite values.
Results may differ from a plain program's by a relative error of at most 0.019.
Values may be sent and summed in bfloat16 or wider, within the bound.
No kernel may reach another device: no remote copies, remote signals or barrier semaphores. Data moves between devices by JAX's collectives and lax.ppermute only.
A program may use at most 192 MiB of HBM per device.

v0:
```python
import jax
import jax.numpy as jnp
from jax import lax
from jax.sharding import PartitionSpec as P

ROUTE_SCALE = 2.5
CONTRACT_ONE = (((1,), (1,)), ((), ()))
CONTRACT_ZERO = (((0,), (0,)), ((), ()))


def swapped(block, axis, apart):
    count = lax.axis_size(axis)
    route = []
    for low in range(count):
        high = low | 1 << apart
        if high != low and high < count:
            route += [(low, high), (high, low)]
    return lax.ppermute(block, axis, route)


def gate_weights(logits, expert_ids, experts):
    match = expert_ids[:, :, None] == jnp.arange(experts, dtype=jnp.int32)[None, None, :]
    picked = jnp.sum(jnp.where(match, logits[:, None, :], 0.0), axis=2)
    sig = jax.nn.sigmoid(picked)
    return ROUTE_SCALE * sig / jnp.sum(sig, axis=1, keepdims=True)


def activations(rows_x, rows_g, w_g, w_u, w_d):
    first = jnp.dot(rows_x, w_g, preferred_element_type=jnp.float32)
    second = jnp.dot(rows_x, w_u, preferred_element_type=jnp.float32)
    sig = jax.nn.sigmoid(first)
    silu = first * sig
    hidden = (silu * second).astype(jnp.bfloat16)
    back = lax.dot_general(rows_g, w_d, CONTRACT_ONE, preferred_element_type=jnp.float32)
    d_first = (back * second * sig * (1.0 + first * (1.0 - sig))).astype(jnp.bfloat16)
    d_second = (back * silu).astype(jnp.bfloat16)
    return (hidden, d_first, d_second)


def weight_grads(rows_x, rows_g, hidden, d_first, d_second):
    own_gate = lax.dot_general(rows_x, d_first, CONTRACT_ZERO, preferred_element_type=jnp.float32)
    own_up = lax.dot_general(rows_x, d_second, CONTRACT_ZERO, preferred_element_type=jnp.float32)
    own_down = lax.dot_general(hidden, rows_g, CONTRACT_ZERO, preferred_element_type=jnp.float32)
    return (
        own_gate.astype(jnp.bfloat16),
        own_up.astype(jnp.bfloat16),
        own_down.astype(jnp.bfloat16),
    )


def slot_pass(rows_x, rows_g, w_g, w_u, w_d):
    hidden, d_first, d_second = activations(rows_x, rows_g, w_g, w_u, w_d)
    out_rows = jnp.dot(hidden, w_d, preferred_element_type=jnp.float32).astype(jnp.bfloat16)
    both = lax.dot_general(d_first, w_g, CONTRACT_ONE, preferred_element_type=jnp.float32)
    both = both + lax.dot_general(d_second, w_u, CONTRACT_ONE, preferred_element_type=jnp.float32)
    grad_rows = both.astype(jnp.bfloat16)
    return (out_rows, grad_rows, weight_grads(rows_x, rows_g, hidden, d_first, d_second))


def per_device(tokens, cotangent, gate_logits, route_slot, slot_expert, w_gate, w_up, w_down):
    tok = tokens.shape[0]
    width = tokens.shape[1]
    top = route_slot.shape[1]
    slots = slot_expert.shape[0]
    experts = gate_logits.shape[1]
    lines = lax.axis_size("local")
    cap = top * tok // lines
    match_slot = route_slot[:, :, None] == jnp.arange(slots, dtype=jnp.int32)[None, None, :]
    expert_ids = jnp.sum(jnp.where(match_slot, slot_expert[None, None, :], 0), axis=2)
    weights, pull_back = jax.vjp(lambda lg: gate_weights(lg, expert_ids, experts), gate_logits)
    scaled = (weights[:, :, None] * cotangent.astype(jnp.float32)[:, None, :]).astype(jnp.bfloat16)
    flat = route_slot.reshape(-1)
    onehot = (flat[:, None] == jnp.arange(slots, dtype=jnp.int32)[None, :]).astype(jnp.int32)
    rank = jnp.sum((jnp.cumsum(onehot, axis=0) - onehot) * onehot, axis=1)
    target = flat * cap + rank
    placer = (jnp.arange(slots * cap, dtype=jnp.int32)[:, None] == target[None, :]).astype(
        jnp.bfloat16
    )
    token_placer = jnp.sum(placer.reshape(slots * cap, tok, top), axis=2)
    x_buffer = jnp.dot(token_placer, tokens, preferred_element_type=jnp.float32).astype(
        jnp.bfloat16
    )
    g_buffer = jnp.dot(
        placer, scaled.reshape(tok * top, width), preferred_element_type=jnp.float32
    ).astype(jnp.bfloat16)
    x_buffer = x_buffer.reshape(lines, 2 * cap, width)
    g_buffer = g_buffer.reshape(lines, 2 * cap, width)
    got_x, got_g = (
        lax.all_to_all(x_buffer, "local", split_axis=0, concat_axis=0, tiled=True),
        lax.all_to_all(g_buffer, "local", split_axis=0, concat_axis=0, tiled=True),
    )
    got_x = got_x.reshape(lines, 2, cap, width)
    got_g = got_g.reshape(lines, 2, cap, width)
    rows_cold_x = got_x[:, 0].reshape(lines * cap, width)
    rows_cold_g = got_g[:, 0].reshape(lines * cap, width)
    rows_hot_x = got_x[:, 1].reshape(lines * cap, width)
    rows_hot_g = got_g[:, 1].reshape(lines * cap, width)
    out_cold, dx_cold, grads_cold = slot_pass(
        rows_cold_x, rows_cold_g, w_gate[0], w_up[0], w_down[0]
    )
    out_hot, dx_hot, grads_hot = slot_pass(rows_hot_x, rows_hot_g, w_gate[1], w_up[1], w_down[1])
    outs_back = jnp.stack(
        [out_cold.reshape(lines, cap, width), out_hot.reshape(lines, cap, width)], axis=1
    )
    dxs_back = jnp.stack(
        [dx_cold.reshape(lines, cap, width), dx_hot.reshape(lines, cap, width)], axis=1
    )
    outs_back = outs_back.reshape(lines, 2 * cap, width)
    dxs_back = dxs_back.reshape(lines, 2 * cap, width)
    home_out, home_dx = (
        lax.all_to_all(outs_back, "local", split_axis=0, concat_axis=0, tiled=True),
        lax.all_to_all(dxs_back, "local", split_axis=0, concat_axis=0, tiled=True),
    )
    home_out = home_out.reshape(slots * cap, width)
    home_dx = home_dx.reshape(slots * cap, width)
    gathered = lax.dot_general(placer, home_out, CONTRACT_ZERO, preferred_element_type=jnp.float32)
    gathered = gathered.reshape(tok, top, width)
    partial_out = jnp.sum(weights[:, :, None] * gathered, axis=1)
    partial_dx = lax.dot_general(
        token_placer, home_dx, CONTRACT_ZERO, preferred_element_type=jnp.float32
    )
    partial_dots = jnp.sum(cotangent.astype(jnp.float32)[:, None, :] * gathered, axis=2)
    mixed, grad_tokens = (
        lax.psum_scatter(
            partial_out.astype(jnp.bfloat16), "group", scatter_dimension=1, tiled=True
        ).astype(jnp.float32),
        lax.psum_scatter(
            partial_dx.astype(jnp.bfloat16), "group", scatter_dimension=1, tiled=True
        ).astype(jnp.float32),
    )
    gate_dots = lax.psum(partial_dots, "group")
    grad_logits = pull_back(gate_dots)[0]
    partner_bit = lax.axis_size("local").bit_length() - 2
    other = swapped((grads_hot[0], grads_hot[1], grads_hot[2]), "local", partner_bit)
    joined = [
        (mine.astype(jnp.float32) + theirs.astype(jnp.float32)).astype(jnp.bfloat16)
        for mine, theirs in zip(grads_hot, other)
    ]
    grad_gate = jnp.stack([grads_cold[0], joined[0]], axis=0)
    grad_up = jnp.stack([grads_cold[1], joined[1]], axis=0)
    grad_down = jnp.stack([grads_cold[2], joined[2]], axis=0)
    return (
        mixed.astype(jnp.bfloat16),
        grad_tokens.astype(jnp.bfloat16),
        grad_logits,
        grad_gate,
        grad_up,
        grad_down,
    )


def solution(mesh):
    return jax.shard_map(
        per_device,
        mesh=mesh,
        in_specs=(
            P("local", None),
            P("local", None),
            P("local", None),
            P("local", None),
            P(),
            P("local", None, "group"),
            P("local", None, "group"),
            P("local", "group", None),
        ),
        out_specs=(
            P("local", "group"),
            P("local", "group"),
            P("local", None),
            P("local", None, "group"),
            P("local", None, "group"),
            P("local", "group", None),
        ),
        check_vma=False,
    )
```

profile of v0, /device:TPU:0, one launch (start us, length us, event | category | flops | bytes accessed | tf_op | source)
XLA Modules:
  0.0 620.1 jit_solution(16297483419287537097)
XLA Ops:
  9.5 5.0 convolution_convert_fusion.1
  14.5 7.3 %all-to-all-start = ((bf16[16,32,7168]{2,1,0:T(8,128)(2,1)}), bf16[16,32,7168]{2,1,0:T(8,128)(2,1)}, u32[]{:S(2)}, u32[]{:S(2)}) async-start(bf16[16,32,7168]{2,1,0:T(8,128)(2,1)} %bitcast.142), calls=%async_computation | async-start | bytes 14680064 | tf_op jit(solution)/shard_map/all_to_all | solution.py:89
  22.9 5.2 convolution_convert_fusion
  28.1 102.3 %all-to-all-done = bf16[16,32,7168]{2,1,0:T(8,128)(2,1)} async-done(((bf16[16,32,7168]{2,1,0:T(8,128)(2,1)}), bf16[16,32,7168]{2,1,0:T(8,128)(2,1)}, u32[]{:S(2)}, u32[]{:S(2)}) %all-to-all-start) | async-done | bytes 7340064 | tf_op jit(solution)/shard_map/all_to_all | solution.py:89
  130.5 5.8 all-to-all-start.2
  136.3 3.8 fusion.60
  148.3 94.5 %all-to-all-done.2 = bf16[16,32,7168]{2,1,0:T(8,128)(2,1)} async-done(((bf16[16,32,7168]{2,1,0:T(8,128)(2,1)}), bf16[16,32,7168]{2,1,0:T(8,128)(2,1)}, u32[]{:S(2)}, u32[]{:S(2)}) %all-to-all-start.2) | async-done | bytes 7340064 | tf_op jit(solution)/shard_map/all_to_all | solution.py:90
  242.8 3.8 fusion.59
  258.0 3.8 pad_maximum_fusion.1
  261.8 4.9 all-to-all-start.3
  266.7 4.2 convolution_convert_fusion.4
  294.9 77.8 %all-to-all-done.3 = bf16[16,32,7168]{2,1,0:T(8,128)(2,1)} async-done(((bf16[16,32,7168]{2,1,0:T(8,128)(2,1)}), bf16[16,32,7168]{2,1,0:T(8,128)(2,1)}, u32[]{:S(2)}, u32[]{:S(2)}) %all-to-all-start.3) | async-done | bytes 7340064 | tf_op jit(solution)/shard_map/all_to_all | solution.py:112
  372.7 10.7 %all-to-all-start.1 = ((bf16[16,32,7168]{2,1,0:T(8,128)(2,1)}), bf16[16,32,7168]{2,1,0:T(8,128)(2,1)}, u32[]{:S(2)}, u32[]{:S(2)}) async-start(bf16[16,32,7168]{2,1,0:T(8,128)(2,1)} %bitcast.144), calls=%async_computation.1 | async-start | bytes 14680064 | tf_op jit(solution)/shard_map/all_to_all | solution.py:111
  383.8 58.0 %collective-permute-done.2 = bf16[128,7168]{1,0:T(8,128)(2,1)} collective-permute-done((bf16[128,7168]{1,0:T(8,128)(2,1)}, bf16[128,7168]{1,0:T(8,128)(2,1)}, u32[]{:S(2)}, u32[]{:S(2)}) %collective-permute-start.2) | collective-permute-done | bytes 1835040 | tf_op jit(solution)/shard_map/ppermute | solution.py:18
  446.5 44.4 %collective-permute-done.1 = bf16[7168,128]{1,0:T(8,128)(2,1)} collective-permute-done((bf16[7168,128]{1,0:T(8,128)(2,1)}, bf16[7168,128]{1,0:T(8,128)(2,1)}, u32[]{:S(2)}, u32[]{:S(2)}) %collective-permute-start.1) | collective-permute-done | bytes 1835040 | tf_op jit(solution)/shard_map/ppermute | solution.py:18
  490.9 3.7 fusion.10
  494.6 35.5 %collective-permute-done = bf16[7168,128]{1,0:T(8,128)(2,1)} collective-permute-done((bf16[7168,128]{1,0:T(8,128)(2,1)S(1)}, bf16[7168,128]{1,0:T(8,128)(2,1)}, u32[]{:S(2)}, u32[]{:S(2)}) %collective-permute-start) | collective-permute-done | bytes 1835040 | tf_op jit(solution)/shard_map/ppermute | solution.py:18
  533.4 4.5 convolution_convert_fusion.10
  539.8 3.7 pad_maximum_fusion.3
  543.5 4.1 all-to-all-done.1
  547.5 7.9 %multiply_reduce_fusion = (f32[32,8]{1,0:T(8,128)S(1)}, bf16[32,7168]{1,0:T(8,128)(2,1)S(1)}) fusion(f32[32,7168]{1,0:T(8,128)S(1)} %convert_element_type.121, f32[32,8]{1,0:T(8,128)S(1)} %copy.51, bf16[512,7168,1]{1,0,2:T(8,128)(2,1)} %bitcast.18, s32[256]{0:T(256)S(1)} %multiply_add_fusion.1), kind=kOutput, calls=%fused_computation.22 | convolution fusion | flops 1886289664 | bytes 8719360 | tf_op jit(solution)/shard_map/dot_general | solution.py:116
  557.4 3.7 pad_maximum_fusion.2
  561.2 14.0 %psum.7 = f32[32,8]{0,1:T(8,128)S(1)} all-reduce(f32[32,8]{0,1:T(8,128)S(1)} %copy.61), channel_id=1, replica_groups=mesh['group'=8,'local'=16] {'group'}, use_global_device_ids=true, to_apply=%region_11.12 | all-reduce | flops 256 | bytes 2048 | tf_op jit(solution)/shard_map/psum | solution.py:131
  578.8 32.8 %reduce-scatter.7.cloned.1.call-done = bf16[896,32]{1,0:T(8,128)(2,1)} async-done(((bf16[7168,32]{1,0:T(8,128)(2,1)}), bf16[896,32]{1,0:T(8,128)(2,1)}) %reduce-scatter.7.cloned.1.call-update) | async-done | bytes 57360
  (102 shorter events, 64.2 us)
Async XLA Ops:
  14.5 7.3 %copy-start.20 = (s32[32]{0:T(128)S(1)}, s32[32]{0:T(128)}, u32[]{:S(2)}) copy-start(s32[32]{0:T(128)} %param.12) | copy-start | bytes 388
  14.5 8.1 %copy-start.19 = (f32[32,24]{0,1:T(8,128)S(1)}, f32[32,24]{0,1:T(8,128)}, u32[]{:S(2)}) copy-start(f32[32,24]{0,1:T(8,128)} %param.10) | copy-start | bytes 9220
  14.5 8.3 %copy-start.18 = (bf16[32,7168]{1,0:T(8,128)(2,1)S(1)}, bf16[32,7168]{1,0:T(8,128)(2,1)}, u32[]{:S(2)}) copy-start(bf16[32,7168]{1,0:T(8,128)(2,1)} %param.9) | copy-start | bytes 1376260
  14.5 116.0 %all-to-all-start = ((bf16[16,32,7168]{2,1,0:T(8,128)(2,1)}), bf16[16,32,7168]{2,1,0:T(8,128)(2,1)}, u32[]{:S(2)}, u32[]{:S(2)}) async-start(bf16[16,32,7168]{2,1,0:T(8,128)(2,1)} %bitcast.142), calls=%async_computation | async-start | bytes 14680064 | tf_op jit(solution)/shard_map/all_to_all | solution.py:89
  130.5 112.4 %all-to-all-start.2 = ((bf16[16,32,7168]{2,1,0:T(8,128)(2,1)}), bf16[16,32,7168]{2,1,0:T(8,128)(2,1)}, u32[]{:S(2)}, u32[]{:S(2)}) async-start(bf16[16,32,7168]{2,1,0:T(8,128)(2,1)} %bitcast.143), calls=%async_computation.2 | async-start | bytes 14680064 | tf_op jit(solution)/shard_map/all_to_all | solution.py:90
  136.3 4.2 copy-start.12
  140.1 5.9 copy-start.4
  140.1 7.0 %copy-start.2 = (bf16[16,1,16,7168]{3,2,1,0:T(8,128)(2,1)}, bf16[16,1,16,7168]{3,2,1,0:T(8,128)(2,1)S(1)}, u32[]{:S(2)}) copy-start(bf16[16,1,16,7168]{3,2,1,0:T(8,128)(2,1)S(1)} %get-tuple-element.10) | copy-start | bytes 11010052
  140.1 4.8 copy-start.14
  242.8 4.2 copy-start.16
  246.6 5.9 copy-start.6
  246.6 5.9 copy-start.8
  246.6 4.8 copy-start.15
  261.8 111.0 %all-to-all-start.3 = ((bf16[16,32,7168]{2,1,0:T(8,128)(2,1)}), bf16[16,32,7168]{2,1,0:T(8,128)(2,1)}, u32[]{:S(2)}, u32[]{:S(2)}) async-start(bf16[16,32,7168]{2,1,0:T(8,128)(2,1)} %bitcast.145), calls=%async_computation.3 | async-start | bytes 14680064 | tf_op jit(solution)/shard_map/all_to_all | solution.py:112
  266.6 7.6 %copy-start.3 = (bf16[16,1,16,7168]{3,2,1,0:T(8,128)(2,1)S(1)}, bf16[16,1,16,7168]{3,2,1,0:T(8,128)(2,1)}, u32[]{:S(2)}) copy-start(bf16[16,1,16,7168]{3,2,1,0:T(8,128)(2,1)} %copy-done.2) | copy-start | bytes 11010052
  270.9 170.9 %collective-permute-start.2 = (bf16[128,7168]{1,0:T(8,128)(2,1)}, bf16[128,7168]{1,0:T(8,128)(2,1)}, u32[]{:S(2)}, u32[]{:S(2)}) collective-permute-start(bf16[128,7168]{1,0:T(8,128)(2,1)} %convolution_convert_fusion.4), channel_id=1, source_target_pairs={{0,8},{8,0},{1,9},{9,1},{2,10},{10,2},{3,11},{11,3},{4,12},{12,4},... | collective-permute-start | bytes 5505032 | tf_op jit(solution)/shard_map/ppermute | solution.py:18
  282.7 6.3 %copy-start.17 = (bf16[2,128,7168]{2,1,0:T(8,128)(2,1)S(1)}, bf16[2,128,7168]{2,1,0:T(8,128)(2,1)}, u32[]{:S(2)}) copy-start(bf16[2,128,7168]{2,1,0:T(8,128)(2,1)} %param.15) | copy-start | bytes 11010052
  285.5 205.4 %collective-permute-start.1 = (bf16[7168,128]{1,0:T(8,128)(2,1)}, bf16[7168,128]{1,0:T(8,128)(2,1)}, u32[]{:S(2)}, u32[]{:S(2)}) collective-permute-start(bf16[7168,128]{1,0:T(8,128)(2,1)} %convolution_convert_fusion.6), channel_id=1, source_target_pairs={{0,8},{8,0},{1,9},{9,1},{2,10},{10,2},{3,11},{11,3},{4,12},{12,4},... | collective-permute-start | bytes 5505032 | tf_op jit(solution)/shard_map/ppermute | solution.py:18
  285.6 244.5 %collective-permute-start = (bf16[7168,128]{1,0:T(8,128)(2,1)S(1)}, bf16[7168,128]{1,0:T(8,128)(2,1)}, u32[]{:S(2)}, u32[]{:S(2)}) collective-permute-start(bf16[7168,128]{1,0:T(8,128)(2,1)S(1)} %convolution_convert_fusion.8), channel_id=1, source_target_pairs={{0,8},{8,0},{1,9},{9,1},{2,10},{10,2},{3,11},{11,3},{4,12},{12,4},... | collective-permute-start | bytes 5505032 | tf_op jit(solution)/shard_map/ppermute | solution.py:18
  372.7 174.8 %all-to-all-start.1 = ((bf16[16,32,7168]{2,1,0:T(8,128)(2,1)}), bf16[16,32,7168]{2,1,0:T(8,128)(2,1)}, u32[]{:S(2)}, u32[]{:S(2)}) async-start(bf16[16,32,7168]{2,1,0:T(8,128)(2,1)} %bitcast.144), calls=%async_computation.1 | async-start | bytes 14680064 | tf_op jit(solution)/shard_map/all_to_all | solution.py:111
  383.5 193.7 %reduce-scatter.9.cloned.1.call-start = ((), (), s32[]{:S(2)}) async-start(), calls=%async_computation.7 | async-start | bytes 2064384
  383.8 60.5 %copy-start.11 = (bf16[1,128,7168]{2,1,0:T(8,128)(2,1)S(1)}, bf16[1,128,7168]{2,1,0:T(8,128)(2,1)}, u32[]{:S(2)}) copy-start(bf16[1,128,7168]{2,1,0:T(8,128)(2,1)} %fusion.4) | copy-start | bytes 5505028
  539.6 72.0 %reduce-scatter.7.cloned.1.call-start = ((), (), s32[]{:S(2)}) async-start(), calls=%async_computation.6 | async-start | bytes 2064384
  557.4 55.9 %copy-start.1 = (bf16[32,7168]{1,0:T(8,128)(2,1)S(1)}, bf16[32,7168]{1,0:T(8,128)(2,1)}, u32[]{:S(2)}) copy-start(bf16[32,7168]{1,0:T(8,128)(2,1)} %param.8) | copy-start | bytes 1376260
  (6 other events, 12.6 us)
Sparse Core Ops, SparseCore 0:
  539.7 37.4 reduce-scatter.8
  579.6 31.9 reduce-scatter.6
where the time goes:
time: 621 us; the launch traced here: 620 us
  waiting for transfers between devices  451 us (73%)
  matrix products  50.6 us (8%)
  starting transfers between devices  36 us (6%)
  other arithmetic  29 us (5%)
  local copies, waits for them, and re-layouts  25.2 us (4%)
  between operations  14.5 us (2%)
  blocking collectives  14 us (2%)
    ppermute x3, waiting for transfers between devices, swapped(): return lax.ppermute(block, axis, route)  138 us
    all_to_all x1, waiting for transfers between devices, per_device(): lax.all_to_all(x_buffer, 'local', split_axis=0, concat_axis=0, tiled=True)  102 us
    all_to_all x1, waiting for transfers between devices, per_device(): lax.all_to_all(g_buffer, 'local', split_axis=0, concat_axis=0, tiled=True)  94.5 us
    all_to_all x1, waiting for transfers between devices, per_device(): lax.all_to_all(dxs_back, 'local', split_axis=0, concat_axis=0, tiled=True)  77.8 us
    unnamed x4, waiting for transfers between devices  34.1 us
    unnamed x47, local copies, waits for them, and re-layouts  17 us
    psum x1, blocking collectives, per_device(): gate_dots = lax.psum(partial_dots, 'group')  14 us
  transfers between devices with their start and end apart: 9, of which 9 were waited for; matrix products, arithmetic and copies ran while one was open for 12% of the time, Pallas kernels for 0%

commit v1 on v0

--- a/solution.py
+++ b/solution.py
@@ -128,7 +128,11 @@
             partial_dx.astype(jnp.bfloat16), "group", scatter_dimension=1, tiled=True
         ).astype(jnp.float32),
     )
-    gate_dots = lax.psum(partial_dots, "group")
+    gate_dots = partial_dots
+    for hop in (1, 2, 4):
+        gate_dots = gate_dots + lax.ppermute(
+            gate_dots, "group", [(dev, dev ^ hop) for dev in range(8)]
+        )
     grad_logits = pull_back(gate_dots)[0]
     partner_bit = lax.axis_size("local").bit_length() - 2
     other = swapped((grads_hot[0], grads_hot[1], grads_hot[2]), "local", partner_bit)

time: 621 us -> 653 us (1.052)
  waiting for transfers between devices: 451 us -> 483 us
  blocking collectives: 14 us -> 0 us
  starting transfers between devices: 36 us -> 49.2 us
    all_to_all x1, waiting for transfers between devices: 4.05 us -> 88 us  [per_device(): lax.all_to_all(outs_back, 'local', split_axis=0, concat_axis=0, tiled=True)]
    all_to_all x1, waiting for transfers between devices: 77.8 us -> 0.01 us  [per_device(): lax.all_to_all(dxs_back, 'local', split_axis=0, concat_axis=0, tiled=True)]
    unnamed x4, waiting for transfers between devices: 34.1 us -> 55.1 us
    psum x1 -> x0, blocking collectives: 14 us -> none  [per_device(): gate_dots = lax.psum(partial_dots, 'group')]
    all_to_all x1, starting transfers between devices: 4.86 us -> 17.9 us  [per_device(): lax.all_to_all(dxs_back, 'local', split_axis=0, concat_axis=0, tiled=True)]
    unnamed x47 -> x49, local copies, waits for them, and re-layouts: 17 us -> 13.4 us
  transfers between devices with their start and end apart: 9 -> 12, of which waited for: 9 -> 7; matrix products, arithmetic and copies ran while one was open for 12% -> 11% of each run, Pallas kernels for 0% -> 0%
where the time goes in v1:
time: 653 us; the launch traced here: 648 us
  waiting for transfers between devices  483 us (74%)
  matrix products  52.4 us (8%)
  starting transfers between devices  49.2 us (8%)
  other arithmetic  27.1 us (4%)
  local copies, waits for them, and re-layouts  21.7 us (3%)
  between operations  14.7 us (2%)
    ppermute x3, waiting for transfers between devices, swapped(): return lax.ppermute(block, axis, route)  143 us
    all_to_all x1, waiting for transfers between devices, per_device(): lax.all_to_all(x_buffer, 'local', split_axis=0, concat_axis=0, tiled=True)  102 us
    all_to_all x1, waiting for transfers between devices, per_device(): lax.all_to_all(g_buffer, 'local', split_axis=0, concat_axis=0, tiled=True)  94.8 us
    all_to_all x1, waiting for transfers between devices, per_device(): lax.all_to_all(outs_back, 'local', split_axis=0, concat_axis=0, tiled=True)  88 us
    unnamed x4, waiting for transfers between devices  55.1 us
    all_to_all x1, starting transfers between devices, per_device(): lax.all_to_all(dxs_back, 'local', split_axis=0, concat_axis=0, tiled=True)  17.9 us
    unnamed x49, local copies, waits for them, and re-layouts  13.4 us
  transfers between devices with their start and end apart: 12, of which 7 were waited for; matrix products, arithmetic and copies ran while one was open for 11% of the time, Pallas kernels for 0%

profile of v1, /device:TPU:0, one launch (start us, length us, event | category | flops | bytes accessed | tf_op | source)
XLA Modules:
  0.0 648.1 jit_solution(7004284631527261739)
XLA Ops:
  9.5 5.0 convolution_convert_fusion.1
  14.5 7.3 %all-to-all-start = ((bf16[16,32,7168]{2,1,0:T(8,128)(2,1)}), bf16[16,32,7168]{2,1,0:T(8,128)(2,1)}, u32[]{:S(2)}, u32[]{:S(2)}) async-start(bf16[16,32,7168]{2,1,0:T(8,128)(2,1)} %bitcast.142), calls=%async_computation | async-start | bytes 14680064 | tf_op jit(solution)/shard_map/all_to_all | solution.py:89
  22.9 5.2 convolution_convert_fusion
  28.1 102.3 %all-to-all-done = bf16[16,32,7168]{2,1,0:T(8,128)(2,1)} async-done(((bf16[16,32,7168]{2,1,0:T(8,128)(2,1)}), bf16[16,32,7168]{2,1,0:T(8,128)(2,1)}, u32[]{:S(2)}, u32[]{:S(2)}) %all-to-all-start) | async-done | bytes 7340064 | tf_op jit(solution)/shard_map/all_to_all | solution.py:89
  130.4 6.1 all-to-all-start.2
  136.6 3.8 fusion.60
  148.6 94.8 %all-to-all-done.2 = bf16[16,32,7168]{2,1,0:T(8,128)(2,1)} async-done(((bf16[16,32,7168]{2,1,0:T(8,128)(2,1)}), bf16[16,32,7168]{2,1,0:T(8,128)(2,1)}, u32[]{:S(2)}, u32[]{:S(2)}) %all-to-all-start.2) | async-done | bytes 7340064 | tf_op jit(solution)/shard_map/all_to_all | solution.py:90
  243.4 3.8 fusion.59
  256.5 4.9 all-to-all-start.1
  261.4 4.1 convolution_convert_fusion.4
  274.6 3.6 pad_maximum_fusion.1
  279.4 88.0 %all-to-all-done.1 = bf16[16,32,7168]{2,1,0:T(8,128)(2,1)} async-done(((bf16[16,32,7168]{2,1,0:T(8,128)(2,1)}), bf16[16,32,7168]{2,1,0:T(8,128)(2,1)}, u32[]{:S(2)}, u32[]{:S(2)}) %all-to-all-start.1) | async-done | bytes 7340064 | tf_op jit(solution)/shard_map/all_to_all | solution.py:111
  367.4 17.9 %all-to-all-start.3 = ((bf16[16,32,7168]{2,1,0:T(8,128)(2,1)}), bf16[16,32,7168]{2,1,0:T(8,128)(2,1)}, u32[]{:S(2)}, u32[]{:S(2)}) async-start(bf16[16,32,7168]{2,1,0:T(8,128)(2,1)} %bitcast.144), calls=%async_computation.3 | async-start | bytes 14680064 | tf_op jit(solution)/shard_map/all_to_all | solution.py:112
  385.4 4.2 fusion.4
  399.3 3.7 fusion.11
  403.1 106.6 %collective-permute-done.4 = bf16[7168,128]{1,0:T(8,128)(2,1)S(1)} collective-permute-done((bf16[7168,128]{1,0:T(8,128)(2,1)S(1)}, bf16[7168,128]{1,0:T(8,128)(2,1)S(1)}, u32[]{:S(2)}, u32[]{:S(2)}) %collective-permute-start.4) | collective-permute-done | bytes 1835040 | tf_op jit(solution)/shard_map/ppermute | solution.py:18
  511.4 36.3 %collective-permute-done.3 = bf16[7168,128]{1,0:T(8,128)(2,1)S(1)} collective-permute-done((bf16[7168,128]{1,0:T(8,128)(2,1)S(1)}, bf16[7168,128]{1,0:T(8,128)(2,1)S(1)}, u32[]{:S(2)}, u32[]{:S(2)}) %collective-permute-start.3) | collective-permute-done | bytes 1835040 | tf_op jit(solution)/shard_map/ppermute | solution.py:18
  549.4 8.7 %multiply_reduce_fusion = (f32[32,8]{1,0:T(8,128)S(1)}, bf16[32,7168]{1,0:T(8,128)(2,1)}) fusion(f32[32,7168]{1,0:T(8,128)S(1)} %convert_element_type.121, f32[32,8]{1,0:T(8,128)S(1)} %copy.51, bf16[512,7168,1]{1,0,2:T(8,128)(2,1)} %bitcast.18, s32[256]{0:T(256)S(1)} %multiply_add_fusion.1), kind=kOutput, calls=%fused_computation.22 | convolution fusion | flops 1886289664 | bytes 8719360 | tf_op jit(solution)/shard_map/dot_general | solution.py:116
  558.2 4.4 convolution_convert_fusion.10
  564.4 4.4 pad_maximum_fusion.4
  574.6 3.7 collective-permute-start.2
  578.3 3.7 pad_maximum_fusion.2
  582.7 22.2 %reduce-scatter.9.cloned.1.call-done = bf16[896,32]{1,0:T(8,128)(2,1)} async-done(((bf16[7168,32]{1,0:T(8,128)(2,1)}), bf16[896,32]{1,0:T(8,128)(2,1)}) %reduce-scatter.9.cloned.1.call-update) | async-done | bytes 57360
  606.6 32.8 %reduce-scatter.7.cloned.1.call-done = bf16[896,32]{1,0:T(8,128)(2,1)} async-done(((bf16[7168,32]{1,0:T(8,128)(2,1)}), bf16[896,32]{1,0:T(8,128)(2,1)}) %reduce-scatter.7.cloned.1.call-update) | async-done | bytes 57360
  (111 shorter events, 55.8 us)
Async XLA Ops:
  14.5 7.3 %copy-start.21 = (s32[32]{0:T(128)S(1)}, s32[32]{0:T(128)}, u32[]{:S(2)}) copy-start(s32[32]{0:T(128)} %param.12) | copy-start | bytes 388
  14.5 8.1 %copy-start.20 = (f32[32,24]{0,1:T(8,128)S(1)}, f32[32,24]{0,1:T(8,128)}, u32[]{:S(2)}) copy-start(f32[32,24]{0,1:T(8,128)} %param.10) | copy-start | bytes 9220
  14.5 8.3 %copy-start.18 = (bf16[32,7168]{1,0:T(8,128)(2,1)S(1)}, bf16[32,7168]{1,0:T(8,128)(2,1)}, u32[]{:S(2)}) copy-start(bf16[32,7168]{1,0:T(8,128)(2,1)} %param.9) | copy-start | bytes 1376260
  14.5 115.9 %all-to-all-start = ((bf16[16,32,7168]{2,1,0:T(8,128)(2,1)}), bf16[16,32,7168]{2,1,0:T(8,128)(2,1)}, u32[]{:S(2)}, u32[]{:S(2)}) async-start(bf16[16,32,7168]{2,1,0:T(8,128)(2,1)} %bitcast.142), calls=%async_computation | async-start | bytes 14680064 | tf_op jit(solution)/shard_map/all_to_all | solution.py:89
  130.4 112.9 %all-to-all-start.2 = ((bf16[16,32,7168]{2,1,0:T(8,128)(2,1)}), bf16[16,32,7168]{2,1,0:T(8,128)(2,1)}, u32[]{:S(2)}, u32[]{:S(2)}) async-start(bf16[16,32,7168]{2,1,0:T(8,128)(2,1)} %bitcast.143), calls=%async_computation.2 | async-start | bytes 14680064 | tf_op jit(solution)/shard_map/all_to_all | solution.py:90
  140.4 5.9 copy-start.4
  140.4 7.0 %copy-start.2 = (bf16[16,1,16,7168]{3,2,1,0:T(8,128)(2,1)}, bf16[16,1,16,7168]{3,2,1,0:T(8,128)(2,1)S(1)}, u32[]{:S(2)}) copy-start(bf16[16,1,16,7168]{3,2,1,0:T(8,128)(2,1)S(1)} %get-tuple-element.10) | copy-start | bytes 11010052
  256.5 110.9 %all-to-all-start.1 = ((bf16[16,32,7168]{2,1,0:T(8,128)(2,1)}), bf16[16,32,7168]{2,1,0:T(8,128)(2,1)}, u32[]{:S(2)}, u32[]{:S(2)}) async-start(bf16[16,32,7168]{2,1,0:T(8,128)(2,1)} %bitcast.145), calls=%async_computation.1 | async-start | bytes 14680064 | tf_op jit(solution)/shard_map/all_to_all | solution.py:111
  261.4 7.7 %copy-start.17 = (bf16[2,7168,128]{2,1,0:T(8,128)(2,1)S(1)}, bf16[2,7168,128]{2,1,0:T(8,128)(2,1)}, u32[]{:S(2)}) copy-start(bf16[2,7168,128]{2,1,0:T(8,128)(2,1)} %param.13) | copy-start | bytes 11010052
  265.6 133.8 %collective-permute-start.5 = (bf16[128,7168]{1,0:T(8,128)(2,1)}, bf16[128,7168]{1,0:T(8,128)(2,1)}, u32[]{:S(2)}, u32[]{:S(2)}) collective-permute-start(bf16[128,7168]{1,0:T(8,128)(2,1)} %convolution_convert_fusion.4), channel_id=1, source_target_pairs={{0,8},{8,0},{1,9},{9,1},{2,10},{10,2},{3,11},{11,3},{4,12},{12,4},... | collective-permute-start | bytes 5505032 | tf_op jit(solution)/shard_map/ppermute | solution.py:18
  367.4 190.7 %all-to-all-start.3 = ((bf16[16,32,7168]{2,1,0:T(8,128)(2,1)}), bf16[16,32,7168]{2,1,0:T(8,128)(2,1)}, u32[]{:S(2)}, u32[]{:S(2)}) async-start(bf16[16,32,7168]{2,1,0:T(8,128)(2,1)} %bitcast.144), calls=%async_computation.3 | async-start | bytes 14680064 | tf_op jit(solution)/shard_map/all_to_all | solution.py:112
  385.3 219.6 %reduce-scatter.9.cloned.1.call-start = ((), (), s32[]{:S(2)}) async-start(), calls=%async_computation.7 | async-start | bytes 2064384
  385.4 7.6 %copy-start.3 = (bf16[16,1,16,7168]{3,2,1,0:T(8,128)(2,1)S(1)}, bf16[16,1,16,7168]{3,2,1,0:T(8,128)(2,1)}, u32[]{:S(2)}) copy-start(bf16[16,1,16,7168]{3,2,1,0:T(8,128)(2,1)} %copy-done.2) | copy-start | bytes 11010052
  389.5 5.9 copy-start.6
  389.5 120.1 %collective-permute-start.4 = (bf16[7168,128]{1,0:T(8,128)(2,1)S(1)}, bf16[7168,128]{1,0:T(8,128)(2,1)S(1)}, u32[]{:S(2)}, u32[]{:S(2)}) collective-permute-start(bf16[7168,128]{1,0:T(8,128)(2,1)S(1)} %convolution_convert_fusion.6), channel_id=1, source_target_pairs={{0,8},{8,0},{1,9},{9,1},{2,10},{10,2},{3,11},{11,3},{4,12},{12,4},... | collective-permute-start | bytes 5505032 | tf_op jit(solution)/shard_map/ppermute | solution.py:18
  399.0 148.7 %collective-permute-start.3 = (bf16[7168,128]{1,0:T(8,128)(2,1)S(1)}, bf16[7168,128]{1,0:T(8,128)(2,1)S(1)}, u32[]{:S(2)}, u32[]{:S(2)}) collective-permute-start(bf16[7168,128]{1,0:T(8,128)(2,1)S(1)} %convolution_convert_fusion.8), channel_id=1, source_target_pairs={{0,8},{8,0},{1,9},{9,1},{2,10},{10,2},{3,11},{11,3},{4,12},{12,4},... | collective-permute-start | bytes 5505032 | tf_op jit(solution)/shard_map/ppermute | solution.py:18
  558.2 10.6 %collective-permute-start = (f32[32,8]{0,1:T(8,128)S(1)}, f32[32,8]{0,1:T(8,128)S(1)}, u32[]{:S(2)}, u32[]{:S(2)}) collective-permute-start(f32[32,8]{0,1:T(8,128)S(1)} %copy.62), channel_id=1, source_target_pairs={{0,16},{16,0},{32,48},{48,32},{64,80},{80,64},{96,112},{112,96},{1... | collective-permute-start | bytes 3080 | tf_op jit(solution)/shard_map/ppermute | solution.py:133
  564.3 6.5 copy-start.10
  564.3 75.0 %reduce-scatter.7.cloned.1.call-start = ((), (), s32[]{:S(2)}) async-start(), calls=%async_computation.6 | async-start | bytes 2064384
  564.4 6.4 copy-start.11
  568.8 5.8 collective-permute-start.1
  572.9 5.4 copy-start.9
  574.6 66.5 %copy-start.1 = (bf16[32,7168]{1,0:T(8,128)(2,1)S(1)}, bf16[32,7168]{1,0:T(8,128)(2,1)}, u32[]{:S(2)}) copy-start(bf16[32,7168]{1,0:T(8,128)(2,1)} %param.8) | copy-start | bytes 1376260
  574.6 7.4 %collective-permute-start.2 = (f32[32,8]{0,1:T(8,128)S(1)}, f32[32,8]{0,1:T(8,128)S(1)}, u32[]{:S(2)}, u32[]{:S(2)}) collective-permute-start(f32[32,8]{0,1:T(8,128)S(1)} %add.69), channel_id=1, source_target_pairs={{0,64},{16,80},{32,96},{48,112},{64,0},{80,16},{96,32},{112,48},{1... | collective-permute-start | bytes 3080 | tf_op jit(solution)/shard_map/ppermute | solution.py:133
  (10 other events, 33.0 us)
Sparse Core Ops, SparseCore 0:
  564.4 40.4 reduce-scatter.8
  607.3 32.0 reduce-scatter.6
